TPU v7x, 32 devices: a whole 2x2x4 slice. The times are simulated.
32 devices in a mesh: line: 4 (over y, core), cross: 8 (over z, x).
Axes of the slice: x: 2, y: 2, z: 4, core: 2. Of those that a mesh axis runs over, the one named last changes fastest.
Arguments:
- jacobian: float32 [5, 5, 128, 1024], P(None, None, 'line', 'cross'), may hold values from -41 to 121, as said below
- time_step: float32 [128, 1024], P('line', 'cross'), may hold values from 2 to 8
- source: bfloat16 [5, 128, 1024], P(None, 'line', 'cross'), may hold values from -12 to 15
- cross_flux: bfloat16 [5, 128, 1024], P(None, 'line', 'cross'), may hold values from -12 to 12
Outputs:
- update: float32 [5, 128, 1024], P(None, 'line', 'cross')
Inputs may be any that keep to these rules, and one draw needn't show every extreme that they name: Every 5 x 5 block of jacobian is symmetric, and for every line the system matrix of the last step has a positive definite symmetric part.
All inputs are finite; a program needn't handle non-finite values.
Results may differ from a plain program's by a relative error of at most 0.0003.
Values may be sent and summed in bfloat16 or wider, within the bound.
A program may use at most 64 MiB of HBM per device.

v0:
```python
import functools

import jax
import jax.numpy as jnp
from jax import lax
from jax.experimental import pallas as pl
from jax.experimental.pallas import tpu as pltpu
from jax.sharding import PartitionSpec as P

NZ = 8
UNK = 5
SUB = 8
STEPS = 4
damping = 0.05
VMEM_BYTES = 60 * 1024 * 1024
MESH = pl.DeviceIdType.MESH


def mm(matrix, operand):
    summed = matrix[:, 0][:, None] * operand[0][None]
    for k in range(1, UNK):
        summed = summed + matrix[:, k][:, None] * operand[k][None]
    return summed


def mv(matrix, vector):
    summed = matrix[:, 0] * vector[0][None]
    for k in range(1, UNK):
        summed = summed + matrix[:, k] * vector[k][None]
    return summed


def inverse(matrix):
    rows = [matrix[i] for i in range(UNK)]
    for k in range(UNK):
        pivot = rows[k]
        scale = 1.0 / pivot[k : k + 1]
        one = jnp.ones_like(scale)
        parts = [pivot[:k]] * (k > 0) + [one] + [pivot[k + 1 :]] * (k < UNK - 1)
        pivot = jnp.concatenate(parts, axis=0) * scale
        rows[k] = pivot
        for i in range(UNK):
            if i == k:
                continue
            row = rows[i]
            factor = row[k : k + 1]
            parts = [row[:k]] * (k > 0) + [jnp.zeros_like(one)] + [row[k + 1 :]] * (k < UNK - 1)
            rows[i] = jnp.concatenate(parts, axis=0) - factor * pivot
    return jnp.stack(rows, axis=0)


def solve_one(matrix, vector):
    rows = [
        jnp.concatenate([matrix[i], vector[i : i + 1]], axis=0) for i in range(UNK)
    ]
    for k in range(UNK):
        pivot = rows[k][1:] * (1.0 / rows[k][:1])
        rows[k] = pivot
        for i in range(UNK):
            if i != k:
                rows[i] = rows[i][1:] - rows[i][:1] * pivot
    return jnp.concatenate(rows, axis=0)


def diagonal_block(values):
    nothing = jnp.zeros_like(values)
    return jnp.stack(
        [jnp.stack([values if i == j else nothing for j in range(UNK)]) for i in range(UNK)]
    )


def kernel(
    line_size, cross_size,
    jac_hbm, step_hbm, source_hbm, flux_hbm, out_ref,
    jac, step, source, flux, res,
    halo_out, halo_in, mats, rhss, last,
    local_sem, halo_send, halo_recv,
    mat_send, mat_recv, rhs_send, rhs_recv, last_send, last_recv,
):
    rounds = line_size.bit_length() - 1
    me = lax.axis_index("line")
    row = lax.axis_index("cross")
    above, below = row + 1, row - 1
    has_above, has_below = row < cross_size - 1, row > 0
    bits = [lax.rem(me // (1 << r), 2) for r in range(rounds)]
    partners = [me + (1 - 2 * bits[r]) * (1 << r) for r in range(rounds)]

    barrier = pltpu.get_barrier_semaphore()
    def greet(target):
        pl.semaphore_signal(barrier, inc=1, device_id=target, device_id_type=MESH)

    @pl.when(has_above)
    def _():
        greet((me, above))

    @pl.when(has_below)
    def _():
        greet((me, below))

    for r in range(rounds):
        greet((partners[r], row))

    loads = [
        pltpu.make_async_copy(src, dst, local_sem.at[i])
        for i, (src, dst) in enumerate(
            [(flux_hbm, flux), (jac_hbm, jac), (step_hbm, step), (source_hbm, source)]
        )
    ]
    for load in loads:
        load.start()

    cells = jac.shape[2]
    lines = jac.shape[3]
    loads[0].wait()
    lane = lax.broadcasted_iota(jnp.int32, (cells, lines), 1)
    tails = jnp.zeros((cells, lines), jnp.float32)
    heads = jnp.zeros((cells, lines), jnp.float32)
    for f in range(UNK):
        field = flux[f].astype(jnp.float32)
        inside = (lane >= NZ * f) & (lane < NZ * (f + 1))
        tails = jnp.where(inside, pltpu.roll(field, NZ * (f + 1), 1), tails)
        heads = jnp.where(inside, field if f == 0 else pltpu.roll(field, NZ * f, 1), heads)
    halo_out[0] = tails.astype(jnp.bfloat16)
    halo_out[1] = heads.astype(jnp.bfloat16)

    def remote(src, dst, send, recv, target):
        return pltpu.make_async_remote_copy(
            src_ref=src, dst_ref=dst, send_sem=send, recv_sem=recv,
            device_id=target, device_id_type=MESH,
        )

    loads[1].wait()
    loads[2].wait()
    sub = lax.broadcasted_iota(jnp.int32, (SUB, lines), 0)
    unit = diagonal_block(jnp.ones((SUB, lines), jnp.float32))
    diag = []
    for t in range(STEPS):
        diag.append(1.0 / step[pl.ds(t, SUB, stride=STEPS), :] + 2.0 * damping)

    def jac_at(t):
        return jac[:, :, pl.ds(t, SUB, stride=STEPS), :]

    def sub_roll(values, shift):
        shift = shift % SUB
        return values if shift == 0 else pltpu.roll(values, shift, values.ndim - 2)

    def upper(block):
        return block * 0.5 - damping * unit

    def lower(block):
        return block * -0.5 - damping * unit

    over1, over2 = 1.0 / diag[1], 1.0 / diag[2]
    up12, low21 = upper(jac_at(2)), lower(jac_at(1))
    up0, low3 = upper(jac_at(1)), lower(jac_at(2))
    schur1 = inverse(diagonal_block(diag[1]) - mm(up12, low21 * over2))
    schur2 = jnp.stack([schur1[:, i] for i in range(UNK)]) * (diag[1] * over2)
    own1 = mm(schur1, lower(jac_at(0)))
    own2 = mm(schur2, upper(jac_at(3)))
    other1 = -mm(up12, own2) * over1
    other2 = -mm(low21, own1) * over2
    head_diag = diagonal_block(diag[0]) - mm(up0, own1)
    head_link = -mm(up0, other1)
    tail_diag = diagonal_block(diag[3]) - mm(low3, own2)
    tail_link = -mm(low3, other2)

    inside_rows = has_above & has_below

    @pl.when(inside_rows)
    def _():
        pl.semaphore_wait(barrier, rounds + 2)

    @pl.when(jnp.logical_not(inside_rows))
    def _():
        pl.semaphore_wait(barrier, rounds + 1)

    up_copy = remote(halo_out.at[0], halo_in.at[0], halo_send.at[0], halo_recv.at[0], (me, above))
    down_copy = remote(halo_out.at[1], halo_in.at[1], halo_send.at[1], halo_recv.at[1], (me, below))

    @pl.when(has_above)
    def _():
        up_copy.start()

    @pl.when(has_below)
    def _():
        down_copy.start()

    even = lax.rem(sub, 2) == 0
    inner_diag = jnp.where(even, tail_diag, head_diag)
    inner_link = jnp.where(even, tail_link, head_link)
    outer_diag = jnp.where(even, head_diag, tail_diag)
    outer_link = jnp.where(even, head_link, tail_link)
    to_next = upper(sub_roll(jac_at(0), -1))
    to_last = lower(sub_roll(jac_at(3), 1))
    levels = []
    half = 1
    while half < SUB:
        left = lax.rem(sub, 2 * half) < half

        def swap(x, left=left):
            return jnp.where(left, sub_roll(x, -1), sub_roll(x, 1))

        def out(x, left=left, half=half):
            return x if half == 1 else jnp.where(
                left, sub_roll(x, 1 - half), sub_roll(x, half - 1)
            )

        couple = jnp.where(left, to_next, to_last)
        inv = inverse(inner_diag)
        through = mm(inv, couple)
        schur = inverse(inner_diag - mm(couple, swap(through)))
        own = mm(schur, inner_link)
        other = -mm(through, swap(own))
        levels.append((half, left, swap, out, inv, couple, schur, own, other, outer_link))
        outer_diag = outer_diag - mm(outer_link, out(own))
        outer_link = -mm(outer_link, out(other))
        inner_diag, inner_link = outer_diag, outer_link
        half *= 2

    def ends(x):
        return x[..., :1, :], x[..., SUB - 1 :, :]

    side = lax.broadcasted_iota(jnp.int32, (2, lines), 0) == 0
    unit2 = diagonal_block(jnp.ones((2, lines), jnp.float32))
    signed = jnp.where(side, 0.5, -0.5)

    def both(first, second):
        shape = first.shape[:-2] + (2, lines)
        return jnp.where(side, jnp.broadcast_to(first, shape), jnp.broadcast_to(second, shape))

    def swap2(x):
        return both(x[..., 1:, :], x[..., :1, :])

    def put(buffer, r, pieces, send, recv):
        for i, piece in enumerate(pieces):
            buffer[r, bits[r], i] = piece
        copy = remote(
            buffer.at[r, bits[r]], buffer.at[r, bits[r]], send.at[r], recv.at[r],
            (partners[r], row),
        )
        copy.start()
        return copy

    group = [
        both(*ends(outer_diag)), both(*ends(outer_link)),
        both(jac[:, :, :1, :], jac[:, :, cells - 1 :, :]),
    ]
    mat_copy = put(mats, 0, group, mat_send, mat_recv)

    loads[3].wait()

    @pl.when(has_below)
    def _():
        up_copy.wait_recv()
        down_copy.wait_send()

    @pl.when(has_above)
    def _():
        down_copy.wait_recv()
        up_copy.wait_send()

    tails = jnp.where(has_below, halo_in[0].astype(jnp.float32), 0.0)
    heads = jnp.where(has_above, halo_in[1].astype(jnp.float32), 0.0)
    for f in range(UNK):
        field = flux[f].astype(jnp.float32)
        tail = tails if f == 0 else pltpu.roll(tails, lines - NZ * f, 1)
        head = pltpu.roll(heads, lines - NZ - NZ * f, 1)
        behind = jnp.where(lane < NZ, tail, pltpu.roll(field, NZ, 1))
        ahead = jnp.where(lane >= lines - NZ, head, pltpu.roll(field, lines - NZ, 1))
        res[f] = source[f].astype(jnp.float32) - 0.5 * (ahead - behind)

    rhs = [res[:, pl.ds(t, SUB, stride=STEPS), :] for t in range(STEPS)]
    y1 = mv(schur1, rhs[1] - mv(up12, rhs[2] * over2))
    y2 = mv(schur2, rhs[2] - mv(low21, rhs[1] * over1))
    head_rhs = rhs[0] - mv(up0, y1)
    tail_rhs = rhs[3] - mv(low3, y2)
    inner_rhs = jnp.where(even, tail_rhs, head_rhs)
    outer_rhs = jnp.where(even, head_rhs, tail_rhs)
    ys = []
    for half, left, swap, out, inv, couple, schur, own, other, link in levels:
        y = mv(schur, inner_rhs - mv(couple, swap(mv(inv, inner_rhs))))
        ys.append(y)
        outer_rhs = outer_rhs - mv(link, out(y))
        inner_rhs = outer_rhs
    ends_rhs = both(*ends(outer_rhs))

    merged = []
    for r in range(rounds - 1):
        if r > 0:
            mat_copy = put(mats, r, group, mat_send, mat_recv)
        rhs_copy = put(rhss, r, [ends_rhs], rhs_send, rhs_recv)
        mat_copy.wait()

        def inner(ref, i):
            return both(ref[r, 0, i][..., 1:, :], ref[r, 1, i][..., :1, :])

        def outer(ref, i):
            return jnp.where(side, ref[r, 0, i], ref[r, 1, i])

        couple = swap2(inner(mats, 2)) * signed - damping * unit2
        diag_in, link_in = inner(mats, 0), inner(mats, 1)
        diag_out, link_out = outer(mats, 0), outer(mats, 1)
        inv = inverse(diag_in)
        through = mm(inv, couple)
        schur = inverse(diag_in - mm(couple, swap2(through)))
        own = mm(schur, link_in)
        other = -mm(through, swap2(own))
        group = [
            diag_out - mm(link_out, own), -mm(link_out, other), outer(mats, 2),
        ]
        rhs_copy.wait()
        rhs_in = inner(rhss, 0)
        y = mv(schur, rhs_in - mv(couple, swap2(mv(inv, rhs_in))))
        ends_rhs = outer(rhss, 0) - mv(link_out, y)
        merged.append((own, other, y))

    final = rounds - 1
    is_left = bits[final] == 0
    inv = inverse(group[0])
    far = mm(inv, group[1])
    far_y = mv(inv, ends_rhs)

    def facing(x):
        return jnp.where(is_left, x[..., 1:, :], x[..., :1, :])

    mine = facing(group[0] - mm(group[1], swap2(far)))
    mine_rhs = facing(ends_rhs - mv(group[1], swap2(far_y)))
    mine_jac = facing(group[2])
    last[bits[final], :UNK] = mine
    last[bits[final], UNK : 2 * UNK] = mine_jac
    last[bits[final], 2 * UNK] = mine_rhs
    last_copy = remote(
        last.at[bits[final]], last.at[bits[final]], last_send, last_recv, (partners[final], row)
    )
    last_copy.start()
    last_copy.wait()
    theirs = 1 - bits[final]
    their_jac = last[theirs, UNK : 2 * UNK]
    unit1 = diagonal_block(jnp.ones((1, lines), jnp.float32))
    my_couple = their_jac * jnp.where(is_left, 0.5, -0.5) - damping * unit1
    their_couple = mine_jac * jnp.where(is_left, -0.5, 0.5) - damping * unit1
    inv = inverse(last[theirs, :UNK])
    meeting = solve_one(
        mine - mm(my_couple, mm(inv, their_couple)),
        mine_rhs - mv(my_couple, mv(inv, last[theirs, 2 * UNK])),
    )
    shape2 = (UNK, 2, lines)
    at_far = far_y - mv(far, jnp.broadcast_to(meeting, shape2))
    x_head = jnp.where(is_left, at_far[:, :1], meeting)
    x_tail = jnp.where(is_left, meeting, at_far[:, 1:])
    for r in reversed(range(rounds - 1)):
        own, other, y = merged[r]
        found = y - mv(own, both(x_head, x_tail)) - mv(other, both(x_tail, x_head))
        x_head, x_tail = (
            jnp.where(bits[r] == 0, x_head, found[:, 1:]),
            jnp.where(bits[r] == 0, found[:, :1], x_tail),
        )

    shape = (UNK, SUB, lines)
    current = jnp.where(
        sub < SUB // 2, jnp.broadcast_to(x_head, shape), jnp.broadcast_to(x_tail, shape)
    )
    for (half, left, swap, out, inv, couple, schur, own, other, link), y in zip(
        reversed(levels), reversed(ys)
    ):
        near = current if half == 1 else jnp.where(
            left, sub_roll(current, half - 1), sub_roll(current, 1 - half)
        )
        away = jnp.where(left, sub_roll(current, -half), sub_roll(current, half))
        found = y - mv(own, near) - mv(other, away)
        if half > 1:
            place = lax.rem(sub, 2 * half)
            current = jnp.where((place == half - 1) | (place == half), found, current)
    x0 = jnp.where(even, current, found)
    x3 = jnp.where(even, found, current)
    x1 = y1 - mv(own1, x0) - mv(other1, x3)
    x2 = y2 - mv(own2, x3) - mv(other2, x0)
    for t, value in enumerate((x0, x1, x2, x3)):
        out_ref[:, pl.ds(t, SUB, stride=STEPS), :] = value


def shards(line_size, cross_size, jacobian, time_step, source, cross_flux):
    cells, lines = time_step.shape
    rounds = line_size.bit_length() - 1
    assert line_size == 1 << rounds and rounds >= 2 and cross_size >= 3
    assert cells == SUB * STEPS
    f32, bf16 = jnp.float32, jnp.bfloat16
    dma = pltpu.SemaphoreType.DMA
    return pl.pallas_call(
        functools.partial(kernel, line_size, cross_size),
        out_shape=pltpu.VMEM((UNK, cells, lines), f32),
        in_specs=[pl.BlockSpec(memory_space=pl.ANY)] * 4,
        out_specs=pl.BlockSpec(memory_space=pltpu.VMEM),
        scratch_shapes=[
            pltpu.VMEM((UNK, UNK, cells, lines), f32),
            pltpu.VMEM((cells, lines), f32),
            pltpu.VMEM((UNK, cells, lines), bf16),
            pltpu.VMEM((UNK, cells, lines), bf16),
            pltpu.VMEM((UNK, cells, lines), f32),
            pltpu.VMEM((2, cells, lines), bf16),
            pltpu.VMEM((2, cells, lines), bf16),
            pltpu.VMEM((rounds - 1, 2, 3, UNK, UNK, 2, lines), f32),
            pltpu.VMEM((rounds - 1, 2, 1, UNK, 2, lines), f32),
            pltpu.VMEM((2, 2 * UNK + 1, UNK, 1, lines), f32),
            dma((4,)),
            dma((2,)), dma((2,)),
            dma((rounds - 1,)), dma((rounds - 1,)),
            dma((rounds - 1,)), dma((rounds - 1,)),
            dma, dma,
        ],
        compiler_params=pltpu.CompilerParams(
            collective_id=0, has_side_effects=True, vmem_limit_bytes=VMEM_BYTES
        ),
        name="sweep",
    )(jacobian, time_step, source, cross_flux)


def solution(mesh):
    placed = (
        P(None, None, "line", "cross"),
        P("line", "cross"),
        P(None, "line", "cross"),
        P(None, "line", "cross"),
    )
    return jax.shard_map(
        functools.partial(shards, mesh.shape["line"], mesh.shape["cross"]),
        mesh=mesh, in_specs=placed, out_specs=P(None, "line", "cross"), check_vma=False,
    )
```

profile of v0, /device:TPU:0, one launch (start us, length us, event | category | flops | bytes accessed | tf_op | source)
XLA Modules:
  0.0 11.8 jit_solution(17501659660640748214)
XLA Ops:
  0.0 11.1 %sweep.1 = f32[5,32,128]{2,1,0:T(8,128)S(1)} custom-call(f32[5,5,32,128]{3,2,1,0:T(8,128)} %jac_hbm.1, f32[32,128]{1,0:T(8,128)} %step_hbm.1, bf16[5,32,128]{2,1,0:T(8,128)(2,1)} %source_hbm.1, bf16[5,32,128]{2,1,0:T(8,128)(2,1)} %flux_hbm.1), custom_call_target="tpu_custom_call" | custom-call | tf_op jit(solution)/shard_map/sweep/pallas_call | solution.py:389
  11.2 0.6 %copy.6 = f32[5,32,128]{2,1,0:T(8,128)} copy(f32[5,32,128]{2,1,0:T(8,128)S(1)} %sweep.1) | data formatting | bytes 163840
where the time goes:
time: 11.9 us; the launch traced here: 11.8 us
  Pallas kernels  11.1 us (93%)
  local copies, waits for them, and re-layouts  0.64 us (5%)
    pallas_call x1, Pallas kernels, shards(): pl.pallas_call(functools.partial(kernel, line_size, cross_size), out_shap...  11.1 us
    unnamed x1, local copies, waits for them, and re-layouts  0.64 us

commit v1 on v0

--- a/solution.py
+++ b/solution.py
@@ -129,6 +129,27 @@
             device_id=target, device_id_type=MESH,
         )
 
+    inside_rows = has_above & has_below
+
+    @pl.when(inside_rows)
+    def _():
+        pl.semaphore_wait(barrier, rounds + 2)
+
+    @pl.when(jnp.logical_not(inside_rows))
+    def _():
+        pl.semaphore_wait(barrier, rounds + 1)
+
+    up_copy = remote(halo_out.at[0], halo_in.at[0], halo_send.at[0], halo_recv.at[0], (me, above))
+    down_copy = remote(halo_out.at[1], halo_in.at[1], halo_send.at[1], halo_recv.at[1], (me, below))
+
+    @pl.when(has_above)
+    def _():
+        up_copy.start()
+
+    @pl.when(has_below)
+    def _():
+        down_copy.start()
+
     loads[1].wait()
     loads[2].wait()
     sub = lax.broadcasted_iota(jnp.int32, (SUB, lines), 0)
@@ -163,27 +184,6 @@
     head_link = -mm(up0, other1)
     tail_diag = diagonal_block(diag[3]) - mm(low3, own2)
     tail_link = -mm(low3, other2)
-
-    inside_rows = has_above & has_below
-
-    @pl.when(inside_rows)
-    def _():
-        pl.semaphore_wait(barrier, rounds + 2)
-
-    @pl.when(jnp.logical_not(inside_rows))
-    def _():
-        pl.semaphore_wait(barrier, rounds + 1)
-
-    up_copy = remote(halo_out.at[0], halo_in.at[0], halo_send.at[0], halo_recv.at[0], (me, above))
-    down_copy = remote(halo_out.at[1], halo_in.at[1], halo_send.at[1], halo_recv.at[1], (me, below))
-
-    @pl.when(has_above)
-    def _():
-        up_copy.start()
-
-    @pl.when(has_below)
-    def _():
-        down_copy.start()
 
     even = lax.rem(sub, 2) == 0
     inner_diag = jnp.where(even, tail_diag, head_diag)

time: 11.9 us -> 11.9 us (level)
  no operation moved by 1% of the time
where the time goes in v1:
time: 11.9 us; the launch traced here: 11.8 us
  Pallas kernels  11.1 us (93%)
  local copies, waits for them, and re-layouts  0.64 us (5%)
    pallas_call x1, Pallas kernels, shards(): pl.pallas_call(functools.partial(kernel, line_size, cross_size), out_shap...  11.1 us
    unnamed x1, local copies, waits for them, and re-layouts  0.64 us

profile of v1, /device:TPU:0, one launch (start us, length us, event | category | flops | bytes accessed | tf_op | source)
XLA Modules:
  0.0 11.8 jit_solution(9865338581414012784)
XLA Ops:
  0.0 11.1 %sweep.1 = f32[5,32,128]{2,1,0:T(8,128)S(1)} custom-call(f32[5,5,32,128]{3,2,1,0:T(8,128)} %jac_hbm.1, f32[32,128]{1,0:T(8,128)} %step_hbm.1, bf16[5,32,128]{2,1,0:T(8,128)(2,1)} %source_hbm.1, bf16[5,32,128]{2,1,0:T(8,128)(2,1)} %flux_hbm.1), custom_call_target="tpu_custom_call" | custom-call | tf_op jit(solution)/shard_map/sweep/pallas_call | solution.py:389
  11.1 0.6 %copy.6 = f32[5,32,128]{2,1,0:T(8,128)} copy(f32[5,32,128]{2,1,0:T(8,128)S(1)} %sweep.1) | data formatting | bytes 163840

commit v2 on v0

--- a/solution.py
+++ b/solution.py
@@ -157,33 +157,33 @@
     schur2 = jnp.stack([schur1[:, i] for i in range(UNK)]) * (diag[1] * over2)
     own1 = mm(schur1, lower(jac_at(0)))
     own2 = mm(schur2, upper(jac_at(3)))
+    inside_rows = has_above & has_below
+
+    @pl.when(inside_rows)
+    def _():
+        pl.semaphore_wait(barrier, rounds + 2)
+
+    @pl.when(jnp.logical_not(inside_rows))
+    def _():
+        pl.semaphore_wait(barrier, rounds + 1)
+
+    up_copy = remote(halo_out.at[0], halo_in.at[0], halo_send.at[0], halo_recv.at[0], (me, above))
+    down_copy = remote(halo_out.at[1], halo_in.at[1], halo_send.at[1], halo_recv.at[1], (me, below))
+
+    @pl.when(has_above)
+    def _():
+        up_copy.start()
+
+    @pl.when(has_below)
+    def _():
+        down_copy.start()
+
     other1 = -mm(up12, own2) * over1
     other2 = -mm(low21, own1) * over2
     head_diag = diagonal_block(diag[0]) - mm(up0, own1)
     head_link = -mm(up0, other1)
     tail_diag = diagonal_block(diag[3]) - mm(low3, own2)
     tail_link = -mm(low3, other2)
-
-    inside_rows = has_above & has_below
-
-    @pl.when(inside_rows)
-    def _():
-        pl.semaphore_wait(barrier, rounds + 2)
-
-    @pl.when(jnp.logical_not(inside_rows))
-    def _():
-        pl.semaphore_wait(barrier, rounds + 1)
-
-    up_copy = remote(halo_out.at[0], halo_in.at[0], halo_send.at[0], halo_recv.at[0], (me, above))
-    down_copy = remote(halo_out.at[1], halo_in.at[1], halo_send.at[1], halo_recv.at[1], (me, below))
-
-    @pl.when(has_above)
-    def _():
-        up_copy.start()
-
-    @pl.when(has_below)
-    def _():
-        down_copy.start()
 
     even = lax.rem(sub, 2) == 0
     inner_diag = jnp.where(even, tail_diag, head_diag)
@@ -333,6 +333,57 @@
         last.at[bits[final]], last.at[bits[final]], last_send, last_recv, (partners[final], row)
     )
     last_copy.start()
+
+    far_end = lax.broadcasted_iota(jnp.int32, (2, lines), 0) == bits[final]
+    base = jnp.where(far_end, far_y, jnp.zeros_like(far_y))
+    slope = jnp.where(far_end, far, -unit2)
+    for r in reversed(range(rounds - 1)):
+        own, other, y = merged[r]
+        found = y - mv(own, base) - mv(other, swap2(base))
+        found_slope = -mm(own, slope) - mm(other, swap2(slope))
+        first = bits[r] == 0
+
+        def keep(old, new, first=first):
+            return both(
+                jnp.where(first, old[..., :1, :], new[..., 1:, :]),
+                jnp.where(first, new[..., :1, :], old[..., 1:, :]),
+            )
+
+        base, slope = keep(base, found), keep(slope, found_slope)
+
+    def spread(x):
+        shape = x.shape[:-2] + (SUB, lines)
+        return jnp.where(
+            sub < SUB // 2,
+            jnp.broadcast_to(x[..., :1, :], shape), jnp.broadcast_to(x[..., 1:, :], shape),
+        )
+
+    base, slope = spread(base), spread(slope)
+    for (half, left, swap, out, inv, couple, schur, own, other, link), y in zip(
+        reversed(levels), reversed(ys)
+    ):
+        def near(x, half=half, left=left):
+            return x if half == 1 else jnp.where(
+                left, sub_roll(x, half - 1), sub_roll(x, 1 - half)
+            )
+
+        def away(x, half=half, left=left):
+            return jnp.where(left, sub_roll(x, -half), sub_roll(x, half))
+
+        found = y - mv(own, near(base)) - mv(other, away(base))
+        found_slope = -mm(own, near(slope)) - mm(other, away(slope))
+        if half > 1:
+            place = lax.rem(sub, 2 * half)
+            filled = (place == half - 1) | (place == half)
+            base = jnp.where(filled, found, base)
+            slope = jnp.where(filled, found_slope, slope)
+    base0, base3 = jnp.where(even, base, found), jnp.where(even, found, base)
+    slope0, slope3 = jnp.where(even, slope, found_slope), jnp.where(even, found_slope, slope)
+    base1 = y1 - mv(own1, base0) - mv(other1, base3)
+    base2 = y2 - mv(own2, base3) - mv(other2, base0)
+    slope1 = -mm(own1, slope0) - mm(other1, slope3)
+    slope2 = -mm(own2, slope3) - mm(other2, slope0)
+
     last_copy.wait()
     theirs = 1 - bits[final]
     their_jac = last[theirs, UNK : 2 * UNK]
@@ -344,39 +395,10 @@
         mine - mm(my_couple, mm(inv, their_couple)),
         mine_rhs - mv(my_couple, mv(inv, last[theirs, 2 * UNK])),
     )
-    shape2 = (UNK, 2, lines)
-    at_far = far_y - mv(far, jnp.broadcast_to(meeting, shape2))
-    x_head = jnp.where(is_left, at_far[:, :1], meeting)
-    x_tail = jnp.where(is_left, meeting, at_far[:, 1:])
-    for r in reversed(range(rounds - 1)):
-        own, other, y = merged[r]
-        found = y - mv(own, both(x_head, x_tail)) - mv(other, both(x_tail, x_head))
-        x_head, x_tail = (
-            jnp.where(bits[r] == 0, x_head, found[:, 1:]),
-            jnp.where(bits[r] == 0, found[:, :1], x_tail),
-        )
-
-    shape = (UNK, SUB, lines)
-    current = jnp.where(
-        sub < SUB // 2, jnp.broadcast_to(x_head, shape), jnp.broadcast_to(x_tail, shape)
-    )
-    for (half, left, swap, out, inv, couple, schur, own, other, link), y in zip(
-        reversed(levels), reversed(ys)
-    ):
-        near = current if half == 1 else jnp.where(
-            left, sub_roll(current, half - 1), sub_roll(current, 1 - half)
-        )
-        away = jnp.where(left, sub_roll(current, -half), sub_roll(current, half))
-        found = y - mv(own, near) - mv(other, away)
-        if half > 1:
-            place = lax.rem(sub, 2 * half)
-            current = jnp.where((place == half - 1) | (place == half), found, current)
-    x0 = jnp.where(even, current, found)
-    x3 = jnp.where(even, found, current)
-    x1 = y1 - mv(own1, x0) - mv(other1, x3)
-    x2 = y2 - mv(own2, x3) - mv(other2, x0)
-    for t, value in enumerate((x0, x1, x2, x3)):
-        out_ref[:, pl.ds(t, SUB, stride=STEPS), :] = value
+    meeting = jnp.broadcast_to(meeting, (UNK, SUB, lines))
+    cells_back = ((base0, slope0), (base1, slope1), (base2, slope2), (base3, slope3))
+    for t, (base, slope) in enumerate(cells_back):
+        out_ref[:, pl.ds(t, SUB, stride=STEPS), :] = base - mv(slope, meeting)
 
 
 def shards(line_size, cross_size, jacobian, time_step, source, cross_flux):

time: 11.9 us -> 12.5 us (1.050)
  Pallas kernels: 11.1 us -> 11.7 us
    pallas_call x1, Pallas kernels: 11.1 us -> 11.7 us  [shards(): pl.pallas_call(functools.partial(kernel, line_size, cross_size), out_shap...]
where the time goes in v2:
time: 12.5 us; the launch traced here: 12.3 us
  Pallas kernels  11.7 us (94%)
  local copies, waits for them, and re-layouts  0.64 us (5%)
    pallas_call x1, Pallas kernels, shards(): pl.pallas_call(functools.partial(kernel, line_size, cross_size), out_shap...  11.7 us
    unnamed x1, local copies, waits for them, and re-layouts  0.64 us

profile of v2, /device:TPU:0, one launch (start us, length us, event | category | flops | bytes accessed | tf_op | source)
XLA Modules:
  0.0 12.3 jit_solution(11544111057238905612)
XLA Ops:
  0.0 11.7 %sweep.1 = f32[5,32,128]{2,1,0:T(8,128)S(1)} custom-call(f32[5,5,32,128]{3,2,1,0:T(8,128)} %jac_hbm.1, f32[32,128]{1,0:T(8,128)} %step_hbm.1, bf16[5,32,128]{2,1,0:T(8,128)(2,1)} %source_hbm.1, bf16[5,32,128]{2,1,0:T(8,128)(2,1)} %flux_hbm.1), custom_call_target="tpu_custom_call" | custom-call | tf_op jit(solution)/shard_map/sweep/pallas_call | solution.py:411
  11.7 0.6 %copy.6 = f32[5,32,128]{2,1,0:T(8,128)} copy(f32[5,32,128]{2,1,0:T(8,128)S(1)} %sweep.1) | data formatting | bytes 163840

commit v3 on v1

--- a/solution.py
+++ b/solution.py
@@ -32,20 +32,36 @@
 
 def inverse(matrix):
     rows = [matrix[i] for i in range(UNK)]
-    for k in range(UNK):
-        pivot = rows[k]
-        scale = 1.0 / pivot[k : k + 1]
-        one = jnp.ones_like(scale)
-        parts = [pivot[:k]] * (k > 0) + [one] + [pivot[k + 1 :]] * (k < UNK - 1)
-        pivot = jnp.concatenate(parts, axis=0) * scale
-        rows[k] = pivot
+    one = jnp.ones_like(rows[0][:1])
+    nothing = jnp.zeros_like(one)
+
+    def with_columns(values, start, pieces):
+        parts = [values[:start]] * (start > 0) + pieces
+        stop = start + len(pieces)
+        parts += [values[stop:]] * (stop < UNK)
+        return jnp.concatenate(parts, axis=0)
+
+    for start in (0, 2):
+        p, q = rows[start], rows[start + 1]
+        a, b = p[start : start + 1], p[start + 1 : start + 2]
+        c, d = q[start : start + 1], q[start + 1 : start + 2]
+        scale = 1.0 / (a * d - b * c)
+        p = with_columns(p, start, [one, nothing])
+        q = with_columns(q, start, [nothing, one])
+        p, q = (d * p - b * q) * scale, (a * q - c * p) * scale
+        rows[start], rows[start + 1] = p, q
         for i in range(UNK):
-            if i == k:
-                continue
-            row = rows[i]
-            factor = row[k : k + 1]
-            parts = [row[:k]] * (k > 0) + [jnp.zeros_like(one)] + [row[k + 1 :]] * (k < UNK - 1)
-            rows[i] = jnp.concatenate(parts, axis=0) - factor * pivot
+            if i not in (start, start + 1):
+                row = rows[i]
+                f, g = row[start : start + 1], row[start + 1 : start + 2]
+                row = with_columns(row, start, [nothing, nothing])
+                rows[i] = row - (f * p + g * q)
+    k = UNK - 1
+    pivot = rows[k]
+    pivot = with_columns(pivot, k, [one]) * (1.0 / pivot[k:])
+    rows[k] = pivot
+    for i in range(k):
+        rows[i] = with_columns(rows[i], k, [nothing]) - rows[i][k:] * pivot
     return jnp.stack(rows, axis=0)
 
 

time: 11.9 us -> 11.9 us (level)
  no operation moved by 1% of the time
where the time goes in v3:
time: 11.9 us; the launch traced here: 11.8 us
  Pallas kernels  11.1 us (93%)
  local copies, waits for them, and re-layouts  0.64 us (5%)
    pallas_call x1, Pallas kernels, shards(): pl.pallas_call(functools.partial(kernel, line_size, cross_size), out_shap...  11.1 us
    unnamed x1, local copies, waits for them, and re-layouts  0.64 us

profile of v3, /device:TPU:0, one launch (start us, length us, event | category | flops | bytes accessed | tf_op | source)
XLA Modules:
  0.0 11.8 jit_solution(15502396824955794037)
XLA Ops:
  0.0 11.1 %sweep.1 = f32[5,32,128]{2,1,0:T(8,128)S(1)} custom-call(f32[5,5,32,128]{3,2,1,0:T(8,128)} %jac_hbm.1, f32[32,128]{1,0:T(8,128)} %step_hbm.1, bf16[5,32,128]{2,1,0:T(8,128)(2,1)} %source_hbm.1, bf16[5,32,128]{2,1,0:T(8,128)(2,1)} %flux_hbm.1), custom_call_target="tpu_custom_call" | custom-call | tf_op jit(solution)/shard_map/sweep/pallas_call | solution.py:405
  11.1 0.6 %copy.6 = f32[5,32,128]{2,1,0:T(8,128)} copy(f32[5,32,128]{2,1,0:T(8,128)S(1)} %sweep.1) | data formatting | bytes 163840

commit v4 on v3

--- a/solution.py
+++ b/solution.py
@@ -145,27 +145,6 @@
             device_id=target, device_id_type=MESH,
         )
 
-    inside_rows = has_above & has_below
-
-    @pl.when(inside_rows)
-    def _():
-        pl.semaphore_wait(barrier, rounds + 2)
-
-    @pl.when(jnp.logical_not(inside_rows))
-    def _():
-        pl.semaphore_wait(barrier, rounds + 1)
-
-    up_copy = remote(halo_out.at[0], halo_in.at[0], halo_send.at[0], halo_recv.at[0], (me, above))
-    down_copy = remote(halo_out.at[1], halo_in.at[1], halo_send.at[1], halo_recv.at[1], (me, below))
-
-    @pl.when(has_above)
-    def _():
-        up_copy.start()
-
-    @pl.when(has_below)
-    def _():
-        down_copy.start()
-
     loads[1].wait()
     loads[2].wait()
     sub = lax.broadcasted_iota(jnp.int32, (SUB, lines), 0)
@@ -200,6 +179,27 @@
     head_link = -mm(up0, other1)
     tail_diag = diagonal_block(diag[3]) - mm(low3, own2)
     tail_link = -mm(low3, other2)
+
+    inside_rows = has_above & has_below
+
+    @pl.when(inside_rows)
+    def _():
+        pl.semaphore_wait(barrier, rounds + 2)
+
+    @pl.when(jnp.logical_not(inside_rows))
+    def _():
+        pl.semaphore_wait(barrier, rounds + 1)
+
+    up_copy = remote(halo_out.at[0], halo_in.at[0], halo_send.at[0], halo_recv.at[0], (me, above))
+    down_copy = remote(halo_out.at[1], halo_in.at[1], halo_send.at[1], halo_recv.at[1], (me, below))
+
+    @pl.when(has_above)
+    def _():
+        up_copy.start()
+
+    @pl.when(has_below)
+    def _():
+        down_copy.start()
 
     even = lax.rem(sub, 2) == 0
     inner_diag = jnp.where(even, tail_diag, head_diag)

time: 11.9 us -> 11.9 us (level)
  no operation moved by 1% of the time
where the time goes in v4:
time: 11.9 us; the launch traced here: 11.8 us
  Pallas kernels  11.1 us (93%)
  local copies, waits for them, and re-layouts  0.64 us (5%)
    pallas_call x1, Pallas kernels, shards(): pl.pallas_call(functools.partial(kernel, line_size, cross_size), out_shap...  11.1 us
    unnamed x1, local copies, waits for them, and re-layouts  0.64 us

profile of v4, /device:TPU:0, one launch (start us, length us, event | category | flops | bytes accessed | tf_op | source)
XLA Modules:
  0.0 11.8 jit_solution(8023722650425874106)
XLA Ops:
  0.0 11.1 %sweep.1 = f32[5,32,128]{2,1,0:T(8,128)S(1)} custom-call(f32[5,5,32,128]{3,2,1,0:T(8,128)} %jac_hbm.1, f32[32,128]{1,0:T(8,128)} %step_hbm.1, bf16[5,32,128]{2,1,0:T(8,128)(2,1)} %source_hbm.1, bf16[5,32,128]{2,1,0:T(8,128)(2,1)} %flux_hbm.1), custom_call_target="tpu_custom_call" | custom-call | tf_op jit(solution)/shard_map/sweep/pallas_call | solution.py:405
  11.1 0.6 %copy.6 = f32[5,32,128]{2,1,0:T(8,128)} copy(f32[5,32,128]{2,1,0:T(8,128)S(1)} %sweep.1) | data formatting | bytes 163840
